TPU v7x, 32 devices: a whole 2x2x4 slice. The times are simulated.
32 devices in a mesh: rep: 2 (over y), mem: 4 (over x, core), grid: 4 (over z).
Axes of the slice: x: 2, y: 2, z: 4, core: 2. Of those that a mesh axis runs over, the one named last changes fastest.
Arguments:
- grid_hidden_state: bfloat16 [8, 1536, 1024], P(('rep', 'mem'), 'grid'), parts along dimension 0, may hold values from -6 to 6
- mesh_node_keys: bfloat16 [8, 512, 1024], P(('rep', 'mem'), 'grid'), parts along dimension 0, may hold values from -6 to 6
- mesh_node_values: bfloat16 [8, 512, 1024], P(('rep', 'mem'), 'grid'), parts along dimension 0, may hold values from -6 to 6
- query_weight: bfloat16 [1024, 1024], replicated, may hold values from -0.1875 to 0.1875
- head_weight: bfloat16 [1024, 100], replicated, may hold values from -0.1875 to 0.1875
- rms_norm_gain: float32 [1024], replicated, may hold values from 0.5 to 1.5
- edge_bias: float32 [3, 16, 1536], P(None, None, 'grid'), may hold values from -6 to 450
- send_rows: int32 [4, 4, 4], P('grid'), may hold values from 0 to 127, as said below
- edge_src: int32 [3, 1536], P(None, 'grid'), may hold values from 0 to 15, as said below
- targets: float32 [200, 1536], P('rep', 'grid'), parts along dimension 0, may hold values from -6 to 6
- point_area_weight: float32 [1536], P('grid'), may hold values from 1 to 10
- variable_loss_weight: float32 [100], replicated, may hold values from 0.5 to 5
Outputs:
- grid_latent_gradient: bfloat16 [8, 1536, 1024], P(('rep', 'mem'), 'grid'), parts along dimension 0
- mesh_key_gradient: bfloat16 [8, 512, 1024], P(('rep', 'mem'), 'grid'), parts along dimension 0
- mesh_value_gradient: bfloat16 [8, 512, 1024], P(('rep', 'mem'), 'grid'), parts along dimension 0
- head_weight_gradient: float32 [8, 1024, 100], P(('rep', 'mem'), 'grid'), parts along dimension 0
There are 2 independent parts, one for each index of `rep`. A program takes and returns all parts, laid end to end along the dimension named above; an argument that names none is the same for every part. Nothing has to cross between parts.
Inputs may be any that keep to these rules, and one draw needn't show every extreme that they name: send_rows[s, d] lists, in its first slots, distinct mesh rows of shard s (indices inside its block of 128) that receiver shard d reads; the other slots hold 0 and no edge reads them; for some receiver shard every slot of every sender is in use. edge_src[k, g] = s * 4 + j names slot j of sender shard s's list for the receiver shard of g; every slot in use is read by some edge of that receiver, no unused slot is read.
All inputs are finite; a program needn't handle non-finite values.
Results may differ from a plain program's by a relative error of at most 0.011.
Values may be sent and summed in bfloat16 or wider, within the bound.
A program may use at most 64 MiB of HBM per device.

v0:
```python
import math

import jax
import jax.numpy as jnp
from jax import lax
from jax.sharding import PartitionSpec as P

H = 16
K = 3


TAU = 0.1
EPS = 1e-06


def soft_sign_value(value):
    return value / jnp.sqrt(value * value + TAU * TAU)


def shards(
    grid_hidden_state,
    mesh_node_keys,
    mesh_node_values,
    query_weight,
    head_weight,
    rms_norm_gain,
    edge_bias,
    send_rows,
    edge_src,
    targets,
    point_area_weight,
    variable_loss_weight,
):
    hidden_state = grid_hidden_state[0]
    own_keys = mesh_node_keys[0]
    own_values = mesh_node_values[0]
    send_table = send_rows[0]
    n_grid = lax.axis_size("grid")
    slot_count = send_table.shape[1]
    points = hidden_state.shape[0]
    features = hidden_state.shape[1]
    head_size = features // H
    flat_table = send_table.reshape(-1)
    out_keys = jnp.take(own_keys, flat_table, axis=0).reshape(n_grid, slot_count, features)
    out_values = jnp.take(own_values, flat_table, axis=0).reshape(n_grid, slot_count, features)
    recv_keys, recv_values = (
        lax.all_to_all(out_keys, "grid", split_axis=0, concat_axis=0, tiled=True),
        lax.all_to_all(out_values, "grid", split_axis=0, concat_axis=0, tiled=True),
    )
    query = jnp.dot(hidden_state, query_weight, preferred_element_type=jnp.float32).astype(
        jnp.bfloat16
    )
    query_heads = query.reshape(points, H, head_size)
    flat_keys = recv_keys.reshape(n_grid * slot_count, features)
    flat_values = recv_values.reshape(n_grid * slot_count, features)
    edge_keys = jnp.take(flat_keys, edge_src, axis=0).reshape(K, points, H, head_size)
    edge_values = jnp.take(flat_values, edge_src, axis=0).reshape(K, points, H, head_size)
    edge_bias_table = jnp.transpose(edge_bias, (0, 2, 1))
    scores = (
        jnp.einsum("ghd,kghd->kgh", query_heads, edge_keys, preferred_element_type=jnp.float32)
        / math.sqrt(head_size)
        + edge_bias_table
    )
    attention_weights = jax.nn.softmax(scores, axis=0)
    attended = jnp.einsum(
        "kgh,kghd->ghd", attention_weights, edge_values, preferred_element_type=jnp.float32
    ).reshape(points, features)
    merged_output = hidden_state.astype(jnp.float32) + attended
    inverse_rms = 1.0 / jnp.sqrt(
        jnp.mean(merged_output * merged_output, axis=1, keepdims=True) + EPS
    )
    normalized_latent = (merged_output * inverse_rms * rms_norm_gain).astype(jnp.bfloat16)
    member_prediction = lax.dot_general(
        head_weight, normalized_latent, (((0,), (1,)), ((), ())), preferred_element_type=jnp.float32
    )
    every_member = lax.all_gather(member_prediction[None], "mem", axis=0, tiled=True)
    member_loss_total = every_member.shape[0]
    pairwise_terms = jnp.sum(soft_sign_value(member_prediction[None] - every_member), axis=0)
    ensemble_spread = soft_sign_value(
        member_prediction - targets
    ) / member_loss_total - pairwise_terms / (member_loss_total * (member_loss_total - 1))
    prediction_gradient = (
        point_area_weight[None, :] * variable_loss_weight[:, None] * ensemble_spread
    ).astype(jnp.bfloat16)
    scale = 1.0 / math.sqrt(points * n_grid)
    head_weight_gradient = lax.psum_scatter(
        lax.dot_general(
            normalized_latent,
            prediction_gradient,
            (((0,), (1,)), ((), ())),
            preferred_element_type=jnp.float32,
        )
        * scale,
        "grid",
        scatter_dimension=0,
        tiled=True,
    )
    grad_normed = lax.dot_general(
        prediction_gradient,
        head_weight,
        (((0,), (1,)), ((), ())),
        preferred_element_type=jnp.float32,
    )
    gained = grad_normed * rms_norm_gain
    grad_combined = inverse_rms * gained - merged_output * inverse_rms**3 * jnp.mean(
        gained * merged_output, axis=1, keepdims=True
    )
    grad_heads = grad_combined.reshape(points, H, head_size)
    grad_weights = jnp.einsum(
        "ghd,kghd->kgh", grad_heads, edge_values, preferred_element_type=jnp.float32
    )
    grad_scores = attention_weights * (
        grad_weights - jnp.sum(attention_weights * grad_weights, axis=0, keepdims=True)
    )
    grad_query = (
        (
            jnp.einsum("kgh,kghd->ghd", grad_scores, edge_keys, preferred_element_type=jnp.float32)
            / math.sqrt(head_size)
        )
        .reshape(points, features)
        .astype(jnp.bfloat16)
    )
    query_float = query_heads.astype(jnp.float32)
    edge_grad_keys = (
        (jnp.einsum("kgh,ghd->kghd", grad_scores, query_float) / math.sqrt(head_size))
        .astype(jnp.bfloat16)
        .reshape(K, points, features)
    )
    edge_grad_values = (
        jnp.einsum("kgh,ghd->kghd", attention_weights, grad_heads)
        .astype(jnp.bfloat16)
        .reshape(K, points, features)
    )
    slot_ids = jnp.arange(n_grid * slot_count, dtype=jnp.int32)
    slot_onehot = (edge_src[:, None, :] == slot_ids[None, :, None]).astype(jnp.bfloat16)
    slot_keys = jnp.einsum(
        "ksg,kgc->sc", slot_onehot, edge_grad_keys, preferred_element_type=jnp.float32
    ).astype(jnp.bfloat16)
    slot_values = jnp.einsum(
        "ksg,kgc->sc", slot_onehot, edge_grad_values, preferred_element_type=jnp.float32
    ).astype(jnp.bfloat16)
    back_keys, back_values = (
        lax.all_to_all(
            slot_keys.reshape(n_grid, slot_count, features),
            "grid",
            split_axis=0,
            concat_axis=0,
            tiled=True,
        ),
        lax.all_to_all(
            slot_values.reshape(n_grid, slot_count, features),
            "grid",
            split_axis=0,
            concat_axis=0,
            tiled=True,
        ),
    )
    grid_latent_gradient = (
        grad_combined
        + lax.dot_general(
            grad_query, query_weight, (((1,), (1,)), ((), ())), preferred_element_type=jnp.float32
        )
    ).astype(jnp.bfloat16)
    mesh_rows = own_keys.shape[0]
    owner_onehot = (flat_table[None, :] == jnp.arange(mesh_rows, dtype=jnp.int32)[:, None]).astype(
        jnp.bfloat16
    )
    mesh_key_gradient = jnp.dot(
        owner_onehot,
        back_keys.reshape(n_grid * slot_count, features),
        preferred_element_type=jnp.float32,
    ).astype(jnp.bfloat16)
    mesh_value_gradient = jnp.dot(
        owner_onehot,
        back_values.reshape(n_grid * slot_count, features),
        preferred_element_type=jnp.float32,
    ).astype(jnp.bfloat16)
    return (
        grid_latent_gradient[None],
        mesh_key_gradient[None],
        mesh_value_gradient[None],
        head_weight_gradient[None],
    )


def solution(mesh):
    placed = (
        P(("rep", "mem"), "grid", None),
        P(("rep", "mem"), "grid", None),
        P(("rep", "mem"), "grid", None),
        P(),
        P(),
        P(),
        P(None, None, "grid"),
        P("grid", None, None),
        P(None, "grid"),
        P("rep", "grid"),
        P("grid"),
        P(),
    )
    return jax.shard_map(
        shards,
        mesh=mesh,
        in_specs=placed,
        out_specs=(
            P(("rep", "mem"), "grid", None),
            P(("rep", "mem"), "grid", None),
            P(("rep", "mem"), "grid", None),
            P(("rep", "mem"), "grid", None),
        ),
        check_vma=False,
    )
```

profile of v0, /device:TPU:0, one launch (start us, length us, event | category | flops | bytes accessed | tf_op | source)
XLA Modules:
  0.0 118.9 jit_solution(16510479423880076977)
XLA Ops:
  7.2 0.0 copy-start
  7.2 0.9 reshape_squeeze.3
  8.1 1.6 %gather_fusion.2 = bf16[16,1024]{1,0:T(8,128)(2,1)S(1)} fusion(bf16[128,1024]{1,0:T(8,128)(2,1)} %bitcast.115, s32[1024]{0:T(1024)S(1)} %pad_clamp_fusion.1), kind=kCustom, calls=%fused_computation.2.clone | custom fusion | bytes 65600 | tf_op jit(solution)/shard_map/jit(_take)/gather | solution.py:45
  9.7 1.6 %gather_fusion = bf16[16,1024]{1,0:T(8,128)(2,1)S(1)} fusion(bf16[128,1024]{1,0:T(8,128)(2,1)} %bitcast.116, s32[1024]{0:T(1024)S(1)} %pad_clamp_fusion.1), kind=kCustom, calls=%fused_computation.clone | custom fusion | bytes 65600 | tf_op jit(solution)/shard_map/jit(_take)/gather | solution.py:44
  11.3 0.1 broadcast_select_fusion.3
  11.4 0.6 reshape.99
  12.0 6.3 %all-to-all-start.1 = ((bf16[4,4,1024]{2,1,0:T(4,128)(2,1)}), bf16[4,4,1024]{2,1,0:T(4,128)(2,1)S(1)}, u32[]{:S(2)}, u32[]{:S(2)}) async-start(bf16[4,4,1024]{2,1,0:T(4,128)(2,1)} %reshape.99), calls=%async_computation.1 | async-start | bytes 65536 | tf_op jit(solution)/shard_map/all_to_all | solution.py:48
  18.4 0.7 compare_select_fusion
  19.1 0.0 copy-done
  19.1 3.0 %convolution_convert_fusion = bf16[384,1024]{1,0:T(8,128)(2,1)} fusion(bf16[1024,1024]{1,0:T(8,128)(2,1)S(1)} %copy-done, bf16[1,384,1024]{2,1,0:T(8,128)(2,1)} %param.16), kind=kOutput, calls=%fused_computation.22 | convolution fusion | flops 805699584 | bytes 3670016 | tf_op jit(solution)/shard_map/dot_general | solution.py:50
  22.1 2.4 %copy.30 = bf16[384,1024]{0,1:T(8,128)(2,1)} copy(bf16[384,1024]{1,0:T(8,128)(2,1)} %convolution_convert_fusion) | data formatting | bytes 1572864 | tf_op jit(solution)/shard_map/convert_element_type | solution.py:50
  24.4 2.4 %bitcast_convert_fusion = f32[384,16,64]{0,2,1:T(8,128)} fusion(bf16[384,1024]{0,1:T(8,128)(2,1)} %copy.30), kind=kLoop, calls=%fused_computation.62 | loop fusion | flops 393216 | bytes 2359296
  26.9 0.0 copy-done.9
  26.9 0.6 reshape.95
  27.5 0.0 all-to-all-done.1
  27.5 5.1 %all-to-all-start = ((bf16[4,4,1024]{2,1,0:T(4,128)(2,1)}), bf16[4,4,1024]{2,1,0:T(4,128)(2,1)S(1)}, u32[]{:S(2)}, u32[]{:S(2)}) async-start(bf16[4,4,1024]{2,1,0:T(4,128)(2,1)} %reshape.95), calls=%async_computation | async-start | bytes 65536 | tf_op jit(solution)/shard_map/all_to_all | solution.py:47
  32.6 0.0 reduce-scatter.2.cloned.1.call-start
  32.6 0.0 copy-done.3
  32.7 1.2 copy.28
  33.8 5.0 %gather_fusion.3 = bf16[1152,1024]{1,0:T(8,128)(2,1)} fusion(bf16[16,1024]{1,0:T(8,128)(2,1)S(1)} %reshape.100, s32[2048]{0:T(1024)S(1)} %pad_clamp_fusion), kind=kCustom, calls=%fused_computation.3.clone | custom fusion | bytes 4723200 | tf_op jit(solution)/shard_map/jit(_take)/gather | solution.py:57
  38.8 4.3 %copy.31 = bf16[3,384,1024]{1,2,0:T(8,128)(2,1)} copy(bf16[3,384,1024]{2,1,0:T(8,128)(2,1)} %bitcast.103) | data formatting | bytes 4718592 | tf_op jit(solution)/shard_map/jit(_take)/gather | solution.py:57
  43.1 0.0 all-to-all-done
  43.1 5.0 %gather_fusion.1 = bf16[1152,1024]{1,0:T(8,128)(2,1)} fusion(bf16[16,1024]{1,0:T(8,128)(2,1)S(1)} %reshape.96, s32[2048]{0:T(1024)S(1)} %pad_clamp_fusion), kind=kCustom, calls=%fused_computation.1.clone | custom fusion | bytes 4723200 | tf_op jit(solution)/shard_map/jit(_take)/gather | solution.py:56
  48.1 4.3 %copy.29 = bf16[3,384,1024]{1,2,0:T(8,128)(2,1)} copy(bf16[3,384,1024]{2,1,0:T(8,128)(2,1)} %bitcast.102) | data formatting | bytes 4718592 | tf_op jit(solution)/shard_map/jit(_take)/gather | solution.py:56
  52.4 4.6 %multiply_reduce_fusion.3 = (f32[384,16,3]{0,1,2:T(8,128)S(1)}, bf16[3,384,1024]{1,2,0:T(8,128)(2,1)}) fusion(f32[384,16,64]{0,2,1:T(8,128)} %bitcast_convert_fusion, bf16[3,384,1024]{1,2,0:T(8,128)(2,1)} %copy.29, pred[3,384]{1,0:T(4,128)(4,1)S(1)} %compare_and_fusion), kind=kLoop, calls=%fused_computation.7 | loop fusion | flops 4700160 | bytes 6366336 | tf_op jit(solution)/shard_map/ghd,kghd->kgh/dot_general | solution.py:60
  57.0 0.0 copy-done.7
  57.1 0.0 copy-done.1
  57.1 0.3 broadcast_select_fusion
  57.4 0.0 copy-start.5
  57.4 0.6 multiply_reduce_fusion.2
  58.0 1.2 %copy-done.2 = f32[384,16,64]{0,2,1:T(8,128)} copy-done((f32[384,16,64]{0,2,1:T(8,128)}, f32[384,16,64]{0,2,1:T(8,128)S(1)}, u32[]{:S(2)}) %copy-start.2) | copy-done | bytes 1572888
  59.2 0.0 copy-done.5
  59.2 0.3 fusion.1
  59.5 3.0 %copy.32 = f32[384,1024]{1,0:T(8,128)} copy(f32[384,1024]{0,1:T(8,128)} %bitcast.101) | data formatting | bytes 3145728 | tf_op jit(solution)/shard_map/reshape | solution.py:67
  62.6 1.7 %multiply_convert_fusion.3 = bf16[384,1024]{1,0:T(8,128)(2,1)S(1)} fusion(f32[1024]{0:T(1024)S(1)} %copy-done.10, f32[384]{0:T(512)S(1)} %get-tuple-element.23, f32[384,1024]{1,0:T(8,128)} %copy.32, bf16[1,384,1024]{2,1,0:T(8,128)(2,1)S(1)} %copy-done.3), kind=kLoop, calls=%fused_computation.19 | loop fusion | flops 1966080 | bytes 3151360 | tf_op jit(solution)/shard_map/convert_element_type | solution.py:72
  64.3 0.0 copy-start.8
  64.3 0.0 copy-start.11
  64.3 0.0 copy-start.12
  64.3 0.4 fusion.18
  64.7 7.8 %all-gather.1 = f32[4,100,384]{2,1,0:T(8,128)S(1)} all-gather(f32[1,100,384]{2,1,0:T(8,128)S(1)} %bitcast.110), channel_id=2, replica_groups=mesh['rep'=2,'mem'=4,'grid'=4] {'mem'}, dimensions={0}, use_global_device_ids=true | all-gather | bytes 768000 | tf_op jit(solution)/shard_map/all_gather | solution.py:76
  72.5 0.1 multiply_reduce_fusion.5
  72.7 0.1 multiply_convert_fusion.4
  72.8 1.0 convolution_multiply_fusion.1
  73.8 3.1 %multiply_reduce_fusion.4 = (f32[384]{0:T(512)S(1)}, f32[384,1024]{1,0:T(8,128)}) fusion(f32[384,1024]{1,0:T(8,128)} %copy.32, bf16[1,384,1024]{2,1,0:T(8,128)(2,1)S(1)} %copy-done.3, f32[1024]{0:T(1024)S(1)} %copy-done.10, bf16[100,384]{1,0:T(8,128)(2,1)S(1)} %multiply_convert_fusion.4, bf16[1024,100]{0,1:T(8,128)(2,1)S(1)} %copy-done.6), kind=kOutput, calls=%fused_computation.18 | convolution fusion | flops 80608896 | bytes 4219392 | tf_op jit(solution)/shard_map/dot_general | solution.py:98
  76.9 0.0 reduce-scatter.2.cloned.1.call-update
  76.9 3.4 %multiply_subtract_fusion = f32[384,1024]{1,0:T(8,128)} fusion(f32[384,1024]{1,0:T(8,128)} %get-tuple-element.27, f32[384]{0:T(512)S(1)} %broadcast_multiply_fusion, f32[384]{0:T(512)S(1)} %get-tuple-element.22, f32[384]{0:T(512)S(1)} %get-tuple-element.23, f32[384,1024]{1,0:T(8,128)} %copy.32, bf16[1,384,1024]{2,1,0:T(8,128)(2,1)S(1)} %copy-done.3), kind=kLoop, calls=%fused_computation.17 | loop fusion | flops 2359296 | bytes 5509632 | tf_op jit(solution)/shard_map/sub | solution.py:105
  80.3 3.1 %copy.33 = f32[384,1024]{0,1:T(8,128)} copy(f32[384,1024]{1,0:T(8,128)} %multiply_subtract_fusion) | data formatting | bytes 3145728 | tf_op jit(solution)/shard_map/sub | solution.py:105
  83.4 3.5 %multiply_convert_fusion = (bf16[384,16,64,3]{0,2,1,3:T(8,128)(2,1)S(1)}, f32[384,16,3]{0,1,2:T(8,128)S(1)}) fusion(f32[384,16,64]{0,2,1:T(8,128)} %bitcast.108, f32[384,16,3]{0,1,2:T(8,128)S(1)} %bitcast.113, bf16[3,384,1024]{1,2,0:T(8,128)(2,1)} %copy.31, pred[3,384]{1,0:T(4,128)(4,1)S(1)} %compare_and_fusion), kind=kLoop, calls=%fused_computation.8 | loop fusion | flops 7059456 | bytes 6440064 | tf_op jit(solution)/shard_map/convert_element_type | solution.py:131
  86.9 0.7 fusion.6
  87.6 0.7 reshape.108
  88.2 5.1 %all-to-all-start.3 = ((bf16[4,4,1024]{2,1,0:T(4,128)(2,1)}), bf16[4,4,1024]{2,1,0:T(4,128)(2,1)S(1)}, u32[]{:S(2)}, u32[]{:S(2)}) async-start(bf16[4,4,1024]{2,1,0:T(4,128)(2,1)} %reshape.108), calls=%async_computation.3 | async-start | bytes 65536 | tf_op jit(solution)/shard_map/all_to_all | solution.py:150
  93.4 2.2 %multiply_convert_fusion.1 = bf16[384,16,64,3]{0,2,1,3:T(8,128)(2,1)S(1)} fusion(f32[384,16,64]{0,2,1:T(8,128)} %bitcast_convert_fusion, f32[384,16,3]{0,1,2:T(8,128)S(1)} %fusion.10), kind=kLoop, calls=%fused_computation.9 | loop fusion | flops 3538944 | bytes 4005888 | tf_op jit(solution)/shard_map/convert_element_type | solution.py:126
  95.6 0.0 copy-done.4
  95.6 0.6 multiply_reduce_fusion
  96.2 0.7 fusion.5
  96.9 0.2 multiply_convert_fusion.2
  97.1 0.6 reshape.105
  97.8 1.2 %all-to-all-done.3 = bf16[4,4,1024]{2,1,0:T(4,128)(2,1)S(1)} async-done(((bf16[4,4,1024]{2,1,0:T(4,128)(2,1)}), bf16[4,4,1024]{2,1,0:T(4,128)(2,1)S(1)}, u32[]{:S(2)}, u32[]{:S(2)}) %all-to-all-start.3) | async-done | bytes 32800 | tf_op jit(solution)/shard_map/all_to_all | solution.py:150
  99.0 3.9 %all-to-all-start.2 = ((bf16[4,4,1024]{2,1,0:T(4,128)(2,1)}), bf16[4,4,1024]{2,1,0:T(4,128)(2,1)S(1)}, u32[]{:S(2)}, u32[]{:S(2)}) async-start(bf16[4,4,1024]{2,1,0:T(4,128)(2,1)} %reshape.105), calls=%async_computation.2 | async-start | bytes 65536 | tf_op jit(solution)/shard_map/all_to_all | solution.py:143
  102.9 3.3 %fusion.2 = bf16[1,384,1024]{2,1,0:T(8,128)(2,1)} fusion(f32[384,1024]{1,0:T(8,128)} %multiply_subtract_fusion, bf16[384,1024]{0,1:T(8,128)(2,1)S(1)} %bitcast.114, bf16[1024,1024]{1,0:T(8,128)(2,1)S(1)} %copy-done), kind=kOutput, calls=%fused_computation.23 | convolution fusion | flops 806092800 | bytes 5242880 | tf_op jit(solution)/shard_map/dot_general | solution.py:160
  106.2 2.3 %all-to-all-done.2 = bf16[4,4,1024]{2,1,0:T(4,128)(2,1)S(1)} async-done(((bf16[4,4,1024]{2,1,0:T(4,128)(2,1)}), bf16[4,4,1024]{2,1,0:T(4,128)(2,1)S(1)}, u32[]{:S(2)}, u32[]{:S(2)}) %all-to-all-start.2) | async-done | bytes 32800 | tf_op jit(solution)/shard_map/all_to_all | solution.py:143
  108.5 0.9 fusion.4
  109.5 0.9 fusion.3
  110.4 1.6 %copy.36 = f32[1,256,100]{1,0,2:T(1,128)} copy(f32[1,256,100]{1,2,0:T(8,128)} %bitcast.117) | data formatting | bytes 204800
  (31 shorter events, 0.2 us)
Async XLA Ops:
  7.2 11.9 %copy-start = (bf16[1024,1024]{1,0:T(8,128)(2,1)S(1)}, bf16[1024,1024]{1,0:T(8,128)(2,1)}, u32[]{:S(2)}) copy-start(bf16[1024,1024]{1,0:T(8,128)(2,1)} %param.19) | copy-start | bytes 6291460
  12.0 15.5 %all-to-all-start.1 = ((bf16[4,4,1024]{2,1,0:T(4,128)(2,1)}), bf16[4,4,1024]{2,1,0:T(4,128)(2,1)S(1)}, u32[]{:S(2)}, u32[]{:S(2)}) async-start(bf16[4,4,1024]{2,1,0:T(4,128)(2,1)} %reshape.99), calls=%async_computation.1 | async-start | bytes 65536 | tf_op jit(solution)/shard_map/all_to_all | solution.py:48
  22.1 4.8 %copy-start.9 = (s32[3,384]{1,0:T(4,128)S(1)}, s32[3,384]{1,0:T(4,128)}, u32[]{:S(2)}) copy-start(s32[3,384]{1,0:T(4,128)} %param.24) | copy-start | bytes 13828
  22.1 10.6 %copy-start.3 = (bf16[1,384,1024]{2,1,0:T(8,128)(2,1)S(1)}, bf16[1,384,1024]{2,1,0:T(8,128)(2,1)}, u32[]{:S(2)}) copy-start(bf16[1,384,1024]{2,1,0:T(8,128)(2,1)} %param.16) | copy-start | bytes 2359300
  27.5 15.5 %all-to-all-start = ((bf16[4,4,1024]{2,1,0:T(4,128)(2,1)}), bf16[4,4,1024]{2,1,0:T(4,128)(2,1)S(1)}, u32[]{:S(2)}, u32[]{:S(2)}) async-start(bf16[4,4,1024]{2,1,0:T(4,128)(2,1)} %reshape.95), calls=%async_computation | async-start | bytes 65536 | tf_op jit(solution)/shard_map/all_to_all | solution.py:47
  32.6 77.7 %reduce-scatter.2.cloned.1.call-start = ((), (), s32[]{:S(2)}) async-start(), calls=%async_computation.5 | async-start | bytes 532480 | tf_op jit(solution)/shard_map/reduce_scatter | solution.py:86
  52.4 4.6 %copy-start.7 = (f32[3,16,384]{2,1,0:T(8,128)S(1)}, f32[3,16,384]{2,1,0:T(8,128)}, u32[]{:S(2)}) copy-start(f32[3,16,384]{2,1,0:T(8,128)} %param.22) | copy-start | bytes 221188
  52.4 4.7 %copy-start.1 = (bf16[3,384,1024]{1,2,0:T(8,128)(2,1)S(1)}, bf16[3,384,1024]{1,2,0:T(8,128)(2,1)}, u32[]{:S(2)}) copy-start(bf16[3,384,1024]{1,2,0:T(8,128)(2,1)} %copy.31) | copy-start | bytes 7077892
  57.4 1.9 %copy-start.5 = (bf16[1,384,1024]{1,2,0:T(8,128)(2,1)S(1)}, bf16[1,384,1024]{1,2,0:T(8,128)(2,1)}, u32[]{:S(2)}) copy-start(bf16[1,384,1024]{1,2,0:T(8,128)(2,1)} %copy.28) | copy-start | bytes 2359300
  58.0 1.2 %copy-start.2 = (f32[384,16,64]{0,2,1:T(8,128)}, f32[384,16,64]{0,2,1:T(8,128)S(1)}, u32[]{:S(2)}) copy-start(f32[384,16,64]{0,2,1:T(8,128)S(1)} %multiply_reduce_fusion.2) | copy-start | bytes 4718596
  59.5 3.0 %copy-start.10 = (f32[1024]{0:T(1024)S(1)}, f32[1024]{0:T(1024)}, u32[]{:S(2)}) copy-start(f32[1024]{0:T(1024)} %param.21) | copy-start | bytes 12292
  62.6 1.7 %copy-start.6 = (bf16[1024,100]{0,1:T(8,128)(2,1)S(1)}, bf16[1024,100]{0,1:T(8,128)(2,1)}, u32[]{:S(2)}) copy-start(bf16[1024,100]{0,1:T(8,128)(2,1)} %param.20) | copy-start | bytes 614404
  64.3 8.3 %copy-start.8 = (f32[100,384]{1,0:T(8,128)S(1)}, f32[100,384]{1,0:T(8,128)}, u32[]{:S(2)}) copy-start(f32[100,384]{1,0:T(8,128)} %param.25) | copy-start | bytes 460804
  64.3 8.3 %copy-start.11 = (f32[384]{0:T(512)S(1)}, f32[384]{0:T(512)}, u32[]{:S(2)}) copy-start(f32[384]{0:T(512)} %param.26) | copy-start | bytes 4612
  64.3 8.3 %copy-start.12 = (f32[100]{0:T(128)S(1)}, f32[100]{0:T(128)}, u32[]{:S(2)}) copy-start(f32[100]{0:T(128)} %param.27) | copy-start | bytes 1204
  88.2 10.7 %all-to-all-start.3 = ((bf16[4,4,1024]{2,1,0:T(4,128)(2,1)}), bf16[4,4,1024]{2,1,0:T(4,128)(2,1)S(1)}, u32[]{:S(2)}, u32[]{:S(2)}) async-start(bf16[4,4,1024]{2,1,0:T(4,128)(2,1)} %reshape.108), calls=%async_computation.3 | async-start | bytes 65536 | tf_op jit(solution)/shard_map/all_to_all | solution.py:150
  93.3 2.2 %copy-start.4 = (bf16[3,384,1024]{1,2,0:T(8,128)(2,1)S(1)}, bf16[3,384,1024]{1,2,0:T(8,128)(2,1)}, u32[]{:S(2)}) copy-start(bf16[3,384,1024]{1,2,0:T(8,128)(2,1)} %get-tuple-element.19) | copy-start | bytes 7077892
  99.0 9.5 %all-to-all-start.2 = ((bf16[4,4,1024]{2,1,0:T(4,128)(2,1)}), bf16[4,4,1024]{2,1,0:T(4,128)(2,1)S(1)}, u32[]{:S(2)}, u32[]{:S(2)}) async-start(bf16[4,4,1024]{2,1,0:T(4,128)(2,1)} %reshape.105), calls=%async_computation.2 | async-start | bytes 65536 | tf_op jit(solution)/shard_map/all_to_all | solution.py:143
Sparse Core Ops, SparseCore 0:
  77.0 21.4 reduce-scatter.1
where the time goes:
time: 120 us; the launch traced here: 119 us
  local copies, waits for them, and re-layouts  37.9 us (32%)
  other arithmetic  20.9 us (17%)
  starting transfers between devices  20.4 us (17%)
  between operations  14.3 us (12%)
  matrix products  14 us (12%)
  blocking collectives  7.8 us (6%)
  waiting for transfers between devices  3.57 us (3%)
    gather x2, local copies, waits for them, and re-layouts, shards(): jnp.take(flat_keys, edge_src, axis=0).reshape(K, points, H, head_size)  9.31 us
    gather x2, local copies, waits for them, and re-layouts, shards(): jnp.take(flat_values, edge_src, axis=0).reshape(K, points, H, head_size)  9.26 us
    all_gather x1, blocking collectives, shards(): lax.all_gather(member_prediction[None], 'mem', axis=0, tiled=True)  7.8 us
    all_to_all x1, starting transfers between devices, shards(): lax.all_to_all(out_values, 'grid', split_axis=0, concat_axis=0, tiled=True)  6.32 us
    all_to_all x1, starting transfers between devices, shards(): lax.all_to_all(out_keys, 'grid', split_axis=0, concat_axis=0, tiled=True)  5.09 us
    all_to_all x1, starting transfers between devices, shards(): lax.all_to_all(slot_values.reshape(n_grid, slot_count, features), 'grid',...  5.09 us
    dot_general x1, other arithmetic, shards(): jnp.einsum('ghd,kghd->kgh', query_heads, edge_keys, preferred_element_typ...  4.57 us
    unnamed x28, local copies, waits for them, and re-layouts  4.08 us
  transfers between devices with their start and end apart: 5, of which 2 were waited for; matrix products, arithmetic and copies ran while one was open for 34% of the time, Pallas kernels for 0%

commit v1 on v0

v1 whole, which is shorter than its diff:
```python
import functools
import math

import jax
import jax.numpy as jnp
from jax import lax
from jax.experimental import pallas as pl
from jax.experimental.pallas import tpu as pltpu
from jax.sharding import PartitionSpec as P

H = 16
K = 3
TAU = 0.1
EPS = 1e-06
LANES = 128
F32 = jnp.float32
BF16 = jnp.bfloat16
MESH = pl.DeviceIdType.MESH


def phi(value):
    return value * lax.rsqrt(value * value + TAU * TAU)


def mm(a, b, ca=1, cb=0):
    return lax.dot_general(a, b, (((ca,), (cb,)), ((), ())), preferred_element_type=F32)


def iota(shape, axis):
    return lax.broadcasted_iota(jnp.int32, shape, axis)


def ring_copies(src, dst, send_sem, recv_sem, axis, me, count):
    copies = []
    for step in range(1, count):
        peer = lax.rem(me + step, count)
        copies.append(
            pltpu.make_async_remote_copy(
                src_ref=src(peer),
                dst_ref=dst(me),
                send_sem=send_sem.at[step],
                recv_sem=recv_sem.at[step],
                device_id={axis: peer},
                device_id_type=MESH,
            )
        )
    return copies


def kernel(
    n,
    m,
    hidden,
    keys,
    values,
    wq,
    hw,
    gain_ref,
    bias,
    send_rows,
    edge_src,
    targets,
    area,
    var_weight,
    out_latent,
    out_keys,
    out_values,
    out_head,
    kv_send,
    kv_recv,
    back_send,
    back_recv,
    f_send,
    f_recv,
    hw_send,
    hw_recv,
    hw_own,
    q_ref,
    hwt,
    rows_ref,
    kb,
    vb,
    kbw,
    score_ref,
    w_ref,
    p_hi,
    p_lo,
    gs_ref,
    combined_ref,
    normed_ref,
    f_ref,
    pg_ref,
    gc_ref,
    gcb_ref,
    kv_sems,
    back_sems,
    f_sems,
    hw_sems,
):
    me = lax.axis_index("grid")
    member = lax.axis_index("mem")
    points, features = hidden.shape[1], hidden.shape[2]
    head = features // H
    per_tile = LANES // head
    cap = send_rows.shape[2]
    pair = 2 * cap
    slots = n * cap
    rows = n * pair
    half = features // 2
    nvar = hw.shape[1]
    vpad = hwt.shape[0]
    mesh_rows = keys.shape[1]
    chunks = points // LANES
    hcols = features // n

    table = send_rows[0].astype(F32).astype(BF16)
    spread_rows = jnp.where(iota((rows, n), 0) // pair == iota((rows, n), 1), 1.0, 0.0).astype(BF16)
    picked = mm(spread_rows, table)
    column = iota((rows, cap), 0) % cap == iota((rows, cap), 1)
    flat = jnp.sum(jnp.where(column, picked, 0.0), axis=1, keepdims=True)
    hit = iota((rows, mesh_rows), 1).astype(F32) == flat
    is_key = iota((rows, mesh_rows), 0) % pair < cap
    pick_key = jnp.where(hit & is_key, 1.0, 0.0).astype(BF16)
    pick_value = jnp.where(hit & ~is_key, 1.0, 0.0).astype(BF16)
    gathered = mm(pick_key, keys[0]) + mm(pick_value, values[0])

    def pack(block):
        return jnp.concatenate([block[:, :half], block[:, half:]], axis=0).astype(BF16)

    for d in range(n):
        kv_send[d] = pack(gathered[d * pair : (d + 1) * pair])

    barrier = pltpu.get_barrier_semaphore()
    for step in range(1, n):
        pl.semaphore_signal(
            barrier, inc=1, device_id={"grid": lax.rem(me + step, n)}, device_id_type=MESH
        )
    for step in range(1, m):
        pl.semaphore_signal(
            barrier, inc=1, device_id={"mem": lax.rem(member + step, m)}, device_id_type=MESH
        )
    pl.semaphore_wait(barrier, n + m - 2)

    kv_copies = ring_copies(
        lambda peer: kv_send.at[peer],
        lambda mine: kv_recv.at[mine],
        kv_sems.at[0],
        kv_sems.at[1],
        "grid",
        me,
        n,
    )
    for copy in kv_copies:
        copy.start()
    kv_recv[me] = kv_send[me]

    q_ref[...] = mm(hidden[0], wq[...]).astype(BF16)
    hwt[...] = jnp.zeros_like(hwt)
    hwt[:nvar, :] = jnp.transpose(hw[...].astype(F32)).astype(BF16)
    kb[...] = jnp.zeros_like(kb)
    vb[...] = jnp.zeros_like(vb)
    gain = gain_ref[...]
    vw = jnp.sum(
        jnp.where(iota((vpad, nvar), 0) == iota((vpad, nvar), 1), var_weight[...], 0.0),
        axis=1,
        keepdims=True,
    )

    for copy in kv_copies:
        copy.wait_recv()
    for s in range(n):
        block = kv_recv[s].astype(F32)
        rows_ref[s * pair : (s + 1) * pair, :half] = block[:pair]
        rows_ref[s * pair : (s + 1) * pair, half:] = block[pair:]
    received = rows_ref[...].astype(BF16)
    slot_at = iota((slots, rows), 0)
    slot_row = slot_at // cap * pair + slot_at % cap
    at_key = jnp.where(iota((slots, rows), 1) == slot_row, 1.0, 0.0).astype(BF16)
    at_value = jnp.where(iota((slots, rows), 1) == slot_row + cap, 1.0, 0.0).astype(BF16)
    slot_k = mm(at_key, received)
    slot_v = mm(at_value, received)
    which = iota((slots, LANES), 1) // head
    for h in range(H):
        tile = slice(h // per_tile * LANES, (h // per_tile + 1) * LANES)
        mine = which == h % per_tile
        kb[h * slots : (h + 1) * slots, tile] = jnp.where(mine, slot_k[:, tile], 0.0).astype(BF16)
        vb[h * slots : (h + 1) * slots, tile] = jnp.where(mine, slot_v[:, tile], 0.0).astype(BF16)

    def onehots(at):
        slot = iota((slots, LANES), 0)
        return [slot == edge_src[k : k + 1, at] for k in range(K)]

    def select(table, hots, at):
        for h in range(H):
            part = table[h * slots : (h + 1) * slots]
            for k in range(K):
                score_ref[k, h : h + 1, at] = jnp.sum(
                    jnp.where(hots[k], part, 0.0), axis=0, keepdims=True
                )

    scale = 1.0 / math.sqrt(head)
    inverse = []
    f_copies = []
    for c in range(chunks):
        at = slice(c * LANES, (c + 1) * LANES)
        hots = onehots(at)
        select(mm(kb[...], q_ref[at, :], 1, 1), hots, at)
        scores = [score_ref[k, :, at] * scale + bias[k, :, at] for k in range(K)]
        top = functools.reduce(jnp.maximum, scores)
        exps = [jnp.exp(s - top) for s in scores]
        total = functools.reduce(jnp.add, exps)
        for k in range(K):
            w_ref[k, :, at] = exps[k] / total
        for h in range(H):
            block = functools.reduce(
                jnp.add,
                [jnp.where(hots[k], w_ref[k, h : h + 1, at], 0.0) for k in range(K)],
            )
            high = block.astype(BF16)
            p_hi[h * slots : (h + 1) * slots, at] = high
            p_lo[h * slots : (h + 1) * slots, at] = (block - high.astype(F32)).astype(BF16)
        attended = mm(p_hi[:, at], vb[...], 0, 0) + mm(p_lo[:, at], vb[...], 0, 0)
        combined = hidden[0, at, :].astype(F32) + attended
        inv = lax.rsqrt(jnp.mean(combined * combined, axis=1, keepdims=True) + EPS)
        inverse.append(inv)
        combined_ref[at, :] = combined
        normed_ref[at, :] = (combined * inv * gain).astype(BF16)
        forecast = mm(hwt[...], normed_ref[at, :], 1, 1)
        f_ref[:, at] = forecast
        f_send[c] = forecast.astype(BF16)
        copies = ring_copies(
            lambda peer, c=c: f_send.at[c],
            lambda mine, c=c: f_recv.at[c, mine],
            f_sems.at[0, c],
            f_sems.at[1, c],
            "mem",
            member,
            m,
        )
        for copy in copies:
            copy.start()
        f_copies.append(copies)

    kbw[...] = mm(kb[...], wq[...], 1, 1).astype(BF16)

    for c in range(chunks):
        at = slice(c * LANES, (c + 1) * LANES)
        for copy in f_copies[c]:
            copy.wait_recv()
        forecast = f_ref[:, at]
        pairwise = jnp.zeros_like(forecast)
        for step in range(1, m):
            other = f_recv[c, lax.rem(member + step, m)].astype(F32)
            pairwise = pairwise + phi(forecast - other)
        pairwise = pairwise[:nvar]
        spread = phi(forecast[:nvar] - targets[:, at]) / m - pairwise / (m * (m - 1))
        pg_ref[:nvar, at] = (area[:, at] * vw[:nvar] * spread).astype(BF16)
        pg_ref[nvar:, at] = jnp.zeros((vpad - nvar, LANES), BF16)

    head_part = mm(pg_ref[...], normed_ref[...]) * (1.0 / math.sqrt(points * n))
    for d in range(n):
        part = head_part[:, d * hcols : (d + 1) * hcols]
        hw_own[d] = part
        hw_send[d] = part.astype(BF16)
    hw_copies = ring_copies(
        lambda peer: hw_send.at[peer],
        lambda mine: hw_recv.at[mine],
        hw_sems.at[0],
        hw_sems.at[1],
        "grid",
        me,
        n,
    )
    for copy in hw_copies:
        copy.start()

    for c in range(chunks):
        at = slice(c * LANES, (c + 1) * LANES)
        hots = onehots(at)
        inv = inverse[c]
        combined = combined_ref[at, :]
        gained = mm(pg_ref[:, at], hwt[...], 0, 0) * gain
        along = jnp.mean(gained * combined, axis=1, keepdims=True)
        grad = inv * gained - combined * (inv * inv * inv * along)
        gc_ref[at, :] = grad
        gcb_ref[at, :] = grad.astype(BF16)
        select(mm(vb[...], gcb_ref[at, :], 1, 1), hots, at)
        grads = [score_ref[k, :, at] for k in range(K)]
        ws = [w_ref[k, :, at] for k in range(K)]
        centre = functools.reduce(jnp.add, [w * g for w, g in zip(ws, grads)])
        for k in range(K):
            score_ref[k, :, at] = ws[k] * (grads[k] - centre) * scale
        for h in range(H):
            block = functools.reduce(
                jnp.add,
                [jnp.where(hots[k], score_ref[k, h : h + 1, at], 0.0) for k in range(K)],
            )
            gs_ref[h * slots : (h + 1) * slots, at] = block.astype(BF16)

    slot_k_grad = mm(gs_ref[...], q_ref[...])
    slot_v_grad = mm(p_hi[...], gcb_ref[...])

    def own_heads(table):
        tiles = []
        for t in range(features // LANES):
            tile = slice(t * LANES, (t + 1) * LANES)
            value = None
            for i in range(per_tile):
                h = t * per_tile + i
                part = table[h * slots : (h + 1) * slots, tile]
                value = part if value is None else jnp.where(which == i, part, value)
            tiles.append(value)
        return jnp.concatenate(tiles, axis=1).astype(BF16)

    back = mm(at_key, own_heads(slot_k_grad), 0, 0) + mm(at_value, own_heads(slot_v_grad), 0, 0)
    for d in range(n):
        back_send[d] = pack(back[d * pair : (d + 1) * pair])
    back_copies = ring_copies(
        lambda peer: back_send.at[peer],
        lambda mine: back_recv.at[mine],
        back_sems.at[0],
        back_sems.at[1],
        "grid",
        me,
        n,
    )
    for copy in back_copies:
        copy.start()
    back_recv[me] = back_send[me]

    for c in range(chunks):
        at = slice(c * LANES, (c + 1) * LANES)
        out_latent[0, at, :] = (gc_ref[at, :] + mm(gs_ref[:, at], kbw[...], 0, 0)).astype(BF16)

    for copy in hw_copies:
        copy.wait_recv()
    total = hw_own[me]
    for step in range(1, n):
        total = total + hw_recv[lax.rem(me + step, n)].astype(F32)
    out_head[0] = jnp.transpose(total)[:, :nvar]

    for copy in back_copies:
        copy.wait_recv()
    for s in range(n):
        block = back_recv[s].astype(F32)
        rows_ref[s * pair : (s + 1) * pair, :half] = block[:pair]
        rows_ref[s * pair : (s + 1) * pair, half:] = block[pair:]
    returned = rows_ref[...].astype(BF16)
    out_keys[0] = mm(pick_key, returned, 0, 0).astype(BF16)
    out_values[0] = mm(pick_value, returned, 0, 0).astype(BF16)

    for copies in [kv_copies, hw_copies, back_copies] + f_copies:
        for copy in copies:
            copy.wait_send()


def shards(
    grid_hidden_state,
    mesh_node_keys,
    mesh_node_values,
    query_weight,
    head_weight,
    rms_norm_gain,
    edge_bias,
    send_rows,
    edge_src,
    targets,
    point_area_weight,
    variable_loss_weight,
):
    n = lax.axis_size("grid")
    m = lax.axis_size("mem")
    points, features = grid_hidden_state.shape[1:]
    nvar = head_weight.shape[1]
    vpad = -(-nvar // 16) * 16
    cap = send_rows.shape[2]
    slots = n * cap
    chunks = points // LANES
    hcols = features // n
    packed = (n, 4 * cap, features // 2)
    vmem = pl.BlockSpec(memory_space=pltpu.VMEM)
    return pl.pallas_call(
        functools.partial(kernel, n, m),
        out_shape=(
            jax.ShapeDtypeStruct((1, points, features), BF16),
            jax.ShapeDtypeStruct(mesh_node_keys.shape, BF16),
            jax.ShapeDtypeStruct(mesh_node_values.shape, BF16),
            jax.ShapeDtypeStruct((1, hcols, nvar), F32),
        ),
        in_specs=[vmem] * 12,
        out_specs=(vmem,) * 4,
        scratch_shapes=[
            pltpu.VMEM(packed, BF16),
            pltpu.VMEM(packed, BF16),
            pltpu.VMEM(packed, BF16),
            pltpu.VMEM(packed, BF16),
            pltpu.VMEM((chunks, vpad, LANES), BF16),
            pltpu.VMEM((chunks, m, vpad, LANES), BF16),
            pltpu.VMEM((n, vpad, hcols), BF16),
            pltpu.VMEM((n, vpad, hcols), BF16),
            pltpu.VMEM((n, vpad, hcols), F32),
            pltpu.VMEM((points, features), BF16),
            pltpu.VMEM((vpad, features), BF16),
            pltpu.VMEM((2 * slots, features), F32),
            pltpu.VMEM((H * slots, features), BF16),
            pltpu.VMEM((H * slots, features), BF16),
            pltpu.VMEM((H * slots, features), BF16),
            pltpu.VMEM((K, H, points), F32),
            pltpu.VMEM((K, H, points), F32),
            pltpu.VMEM((H * slots, points), BF16),
            pltpu.VMEM((H * slots, points), BF16),
            pltpu.VMEM((H * slots, points), BF16),
            pltpu.VMEM((points, features), F32),
            pltpu.VMEM((points, features), BF16),
            pltpu.VMEM((vpad, points), F32),
            pltpu.VMEM((vpad, points), BF16),
            pltpu.VMEM((points, features), F32),
            pltpu.VMEM((points, features), BF16),
            pltpu.SemaphoreType.DMA((2, n)),
            pltpu.SemaphoreType.DMA((2, n)),
            pltpu.SemaphoreType.DMA((2, chunks, m)),
            pltpu.SemaphoreType.DMA((2, n)),
        ],
        compiler_params=pltpu.CompilerParams(
            collective_id=0, has_side_effects=True, vmem_limit_bytes=56 * 1024 * 1024
        ),
    )(
        grid_hidden_state,
        mesh_node_keys,
        mesh_node_values,
        query_weight,
        head_weight,
        rms_norm_gain.reshape(1, features),
        edge_bias,
        send_rows,
        edge_src,
        targets,
        point_area_weight.reshape(1, points),
        variable_loss_weight.reshape(1, nvar),
    )


def solution(mesh):
    placed = (
        P(("rep", "mem"), "grid", None),
        P(("rep", "mem"), "grid", None),
        P(("rep", "mem"), "grid", None),
        P(),
        P(),
        P(),
        P(None, None, "grid"),
        P("grid", None, None),
        P(None, "grid"),
        P("rep", "grid"),
        P("grid"),
        P(),
    )
    return jax.shard_map(
        shards,
        mesh=mesh,
        in_specs=placed,
        out_specs=(P(("rep", "mem"), "grid", None),) * 4,
        check_vma=False,
    )
```

time: 120 us -> 39 us (0.33)
  Pallas kernels: 0 us -> 28.9 us
  local copies, waits for them, and re-layouts: 37.9 us -> 9.16 us
  other arithmetic: 20.9 us -> 0 us
  starting transfers between devices: 20.4 us -> 0 us
  matrix products: 14 us -> 0 us
  between operations: 14.3 us -> 0.65 us
  blocking collectives: 7.8 us -> 0 us
  waiting for transfers between devices: 3.57 us -> 0 us
    pallas_call x0 -> x1, Pallas kernels: none -> 28.9 us  [shards(): pl.pallas_call(functools.partial(kernel, n, m), out_shape=(jax.ShapeDtype...]
    gather x6 -> x0, local copies, waits for them, and re-layouts: 21.8 us -> none  [the longest x2 9.31 us: shards(): jnp.take(flat_keys, edge_src, axis=0).reshape(K, points, H, head_size)]
    all_to_all x4 -> x0, starting transfers between devices: 20.4 us -> none  [the longest x1 6.32 us: shards(): lax.all_to_all(out_values, 'grid', split_axis=0, concat_axis=0, tiled=True)]
    dot_general x9 -> x0, matrix products: 14 us -> none  [the longest x1 3.32 us: shards(): lax.dot_general(grad_query, query_weight, (((1,), (1,)), ((), ())), prefe...]
    all_gather x1 -> x0, blocking collectives: 7.8 us -> none  [shards(): lax.all_gather(member_prediction[None], 'mem', axis=0, tiled=True)]
    convert_element_type x5 -> x0, other arithmetic: 7.65 us -> none  [the longest x1 3.46 us: shards(): edge_grad_values = jnp.einsum('kgh,ghd->kghd', attention_weights, grad_he...]
    dot_general x3 -> x0, other arithmetic: 5.81 us -> none  [the longest x1 4.57 us: shards(): jnp.einsum('ghd,kghd->kgh', query_heads, edge_keys, preferred_element_typ...]
    reshape x9 -> x1, local copies, waits for them, and re-layouts: 5.65 us -> 1.25 us  [shards(): point_area_weight.reshape(1, points)]
  transfers between devices with their start and end apart: 5 -> 0, of which waited for: 2 -> 0; matrix products, arithmetic and copies ran while one was open for 34% -> 0% of each run, Pallas kernels for 0% -> 0%
where the time goes in v1:
time: 39 us; the launch traced here: 38.7 us
  Pallas kernels  28.9 us (74%)
  local copies, waits for them, and re-layouts  9.16 us (23%)
  between operations  0.65 us (2%)
    pallas_call x1, Pallas kernels, shards(): pl.pallas_call(functools.partial(kernel, n, m), out_shape=(jax.ShapeDtype...  28.9 us
    unnamed x6, local copies, waits for them, and re-layouts  6.23 us
    pallas_call x1, local copies, waits for them, and re-layouts, shards(): pl.pallas_call(functools.partial(kernel, n, m), out_shape=(jax.ShapeDtype...  1.69 us
    reshape x1, local copies, waits for them, and re-layouts, shards(): point_area_weight.reshape(1, points)  1.25 us

profile of v1, /device:TPU:0, one launch (start us, length us, event | category | flops | bytes accessed | tf_op | source)
XLA Modules:
  0.0 38.7 jit_solution(5006902732547969852)
XLA Ops:
  0.6 1.2 %reshape.18.area = f32[1,384]{1,0:T(1,128)} reshape(f32[384]{0:T(512)} %param.22) | data formatting | bytes 3072 | tf_op jit(solution)/shard_map/reshape | solution.py:438
  1.9 1.8 %copy.16.hw = bf16[1024,100]{1,0:T(8,128)(2,1)} copy(bf16[1024,100]{0,1:T(8,128)(2,1)} %param.16) | data formatting | bytes 409600 | tf_op args[4]
  3.7 28.9 %shard_map.147 = (bf16[1,384,1024]{2,1,0:T(8,128)(2,1)}, bf16[1,128,1024]{2,1,0:T(8,128)(2,1)}, bf16[1,128,1024]{2,1,0:T(8,128)(2,1)}, f32[1,256,100]{2,1,0:T(8,128)}) custom-call(bf16[1,384,1024]{2,1,0:T(8,128)(2,1)} %hidden.1, bf16[1,128,1024]{2,1,0:T(8,128)(2,1)} %keys.1, bf16[1,128,1024]{2,1,0:T(8,128)(2,1)} %values.1, bf16[1024,1024]{1,0:T(8,128)(2,1)} %wq.1, ...), custom_call_target="tpu_custom_call" | custom-call | tf_op jit(solution)/shard_map/pallas_call | solution.py:382
  32.6 0.0 copy-start
  32.6 1.7 %copy.17 = f32[1,256,100]{1,0,2:T(1,128)} copy(f32[1,256,100]{2,1,0:T(8,128)} %get-tuple-element.7) | data formatting | bytes 204800 | tf_op jit(solution)/shard_map/pallas_call | solution.py:382
  34.3 2.1 %copy.21 = bf16[1,384,1024]{2,1,0:T(8,128)(2,1)} copy(bf16[1,384,1024]{2,1,0:T(8,128)(2,1)} %get-tuple-element.12) | data formatting | bytes 1572864
  36.4 1.7 %copy.22 = bf16[1,128,1024]{2,1,0:T(8,128)(2,1)} copy(bf16[1,128,1024]{2,1,0:T(8,128)(2,1)} %get-tuple-element.13) | data formatting | bytes 524288
  38.0 0.0 copy-done
  38.0 0.7 %copy.23 = bf16[1,128,1024]{2,1,0:T(8,128)(2,1)} copy(bf16[1,128,1024]{2,1,0:T(8,128)(2,1)S(1)} %copy-done) | data formatting | bytes 524288
Async XLA Ops:
  32.6 5.4 %copy-start = (bf16[1,128,1024]{2,1,0:T(8,128)(2,1)S(1)}, bf16[1,128,1024]{2,1,0:T(8,128)(2,1)}, u32[]{:S(2)}) copy-start(bf16[1,128,1024]{2,1,0:T(8,128)(2,1)} %get-tuple-element.14) | copy-start | bytes 786436

commit v2 on v1

--- a/solution.py
+++ b/solution.py
@@ -50,10 +50,10 @@
 def kernel(
     n,
     m,
-    hidden,
+    hidden_in,
     keys,
     values,
-    wq,
+    wq_in,
     hw,
     gain_ref,
     bias,
@@ -63,9 +63,13 @@
     area,
     var_weight,
     out_latent,
-    out_keys,
-    out_values,
+    out_returned,
+    out_picks,
     out_head,
+    hidden,
+    wq,
+    latent,
+    local_sems,
     kv_send,
     kv_recv,
     back_send,
@@ -107,11 +111,25 @@
     slots = n * cap
     rows = n * pair
     half = features // 2
-    nvar = hw.shape[1]
+    nvar = hw.shape[0]
     vpad = hwt.shape[0]
     mesh_rows = keys.shape[1]
     chunks = points // LANES
     hcols = features // n
+
+    barrier = pltpu.get_barrier_semaphore()
+    for step in range(1, n):
+        pl.semaphore_signal(
+            barrier, inc=1, device_id={"grid": lax.rem(me + step, n)}, device_id_type=MESH
+        )
+    for step in range(1, m):
+        pl.semaphore_signal(
+            barrier, inc=1, device_id={"mem": lax.rem(member + step, m)}, device_id_type=MESH
+        )
+    load_hidden = pltpu.make_async_copy(hidden_in, hidden, local_sems.at[0])
+    load_wq = pltpu.make_async_copy(wq_in, wq, local_sems.at[1])
+    load_hidden.start()
+    load_wq.start()
 
     table = send_rows[0].astype(F32).astype(BF16)
     spread_rows = jnp.where(iota((rows, n), 0) // pair == iota((rows, n), 1), 1.0, 0.0).astype(BF16)
@@ -130,15 +148,6 @@
     for d in range(n):
         kv_send[d] = pack(gathered[d * pair : (d + 1) * pair])
 
-    barrier = pltpu.get_barrier_semaphore()
-    for step in range(1, n):
-        pl.semaphore_signal(
-            barrier, inc=1, device_id={"grid": lax.rem(me + step, n)}, device_id_type=MESH
-        )
-    for step in range(1, m):
-        pl.semaphore_signal(
-            barrier, inc=1, device_id={"mem": lax.rem(member + step, m)}, device_id_type=MESH
-        )
     pl.semaphore_wait(barrier, n + m - 2)
 
     kv_copies = ring_copies(
@@ -154,17 +163,22 @@
         copy.start()
     kv_recv[me] = kv_send[me]
 
-    q_ref[...] = mm(hidden[0], wq[...]).astype(BF16)
     hwt[...] = jnp.zeros_like(hwt)
-    hwt[:nvar, :] = jnp.transpose(hw[...].astype(F32)).astype(BF16)
+    hwt[:nvar, :] = hw[...]
     kb[...] = jnp.zeros_like(kb)
     vb[...] = jnp.zeros_like(vb)
     gain = gain_ref[...]
+    area_row = area[...].reshape(1, points)
+    out_picks[...] = jnp.concatenate([pick_key, pick_value], axis=0)
     vw = jnp.sum(
         jnp.where(iota((vpad, nvar), 0) == iota((vpad, nvar), 1), var_weight[...], 0.0),
         axis=1,
         keepdims=True,
     )
+
+    load_hidden.wait()
+    load_wq.wait()
+    q_ref[...] = mm(hidden[0], wq[...]).astype(BF16)
 
     for copy in kv_copies:
         copy.wait_recv()
@@ -254,7 +268,7 @@
             pairwise = pairwise + phi(forecast - other)
         pairwise = pairwise[:nvar]
         spread = phi(forecast[:nvar] - targets[:, at]) / m - pairwise / (m * (m - 1))
-        pg_ref[:nvar, at] = (area[:, at] * vw[:nvar] * spread).astype(BF16)
+        pg_ref[:nvar, at] = (area_row[:, at] * vw[:nvar] * spread).astype(BF16)
         pg_ref[nvar:, at] = jnp.zeros((vpad - nvar, LANES), BF16)
 
     head_part = mm(pg_ref[...], normed_ref[...]) * (1.0 / math.sqrt(points * n))
@@ -330,14 +344,17 @@
 
     for c in range(chunks):
         at = slice(c * LANES, (c + 1) * LANES)
-        out_latent[0, at, :] = (gc_ref[at, :] + mm(gs_ref[:, at], kbw[...], 0, 0)).astype(BF16)
+        latent[0, at, :] = (gc_ref[at, :] + mm(gs_ref[:, at], kbw[...], 0, 0)).astype(BF16)
+
+    store_latent = pltpu.make_async_copy(latent, out_latent, local_sems.at[2])
+    store_latent.start()
 
     for copy in hw_copies:
         copy.wait_recv()
     total = hw_own[me]
     for step in range(1, n):
         total = total + hw_recv[lax.rem(me + step, n)].astype(F32)
-    out_head[0] = jnp.transpose(total)[:, :nvar]
+    out_head[:, 0, :] = total[:nvar]
 
     for copy in back_copies:
         copy.wait_recv()
@@ -345,13 +362,26 @@
         block = back_recv[s].astype(F32)
         rows_ref[s * pair : (s + 1) * pair, :half] = block[:pair]
         rows_ref[s * pair : (s + 1) * pair, half:] = block[pair:]
-    returned = rows_ref[...].astype(BF16)
-    out_keys[0] = mm(pick_key, returned, 0, 0).astype(BF16)
-    out_values[0] = mm(pick_value, returned, 0, 0).astype(BF16)
-
+    out_returned[...] = rows_ref[...].astype(BF16)
+
+    store_latent.wait()
     for copies in [kv_copies, hw_copies, back_copies] + f_copies:
         for copy in copies:
             copy.wait_send()
+
+
+def finish(latent, returned, picks, head, out_latent, out_keys, out_values, out_head, sems):
+    copies = [
+        pltpu.make_async_copy(latent, out_latent, sems.at[0]),
+        pltpu.make_async_copy(head, out_head, sems.at[1]),
+    ]
+    for copy in copies:
+        copy.start()
+    rows = returned.shape[0]
+    out_keys[0] = mm(picks[:rows], returned[...], 0, 0).astype(BF16)
+    out_values[0] = mm(picks[rows:], returned[...], 0, 0).astype(BF16)
+    for copy in copies:
+        copy.wait()
 
 
 def shards(
@@ -372,6 +402,7 @@
     m = lax.axis_size("mem")
     points, features = grid_hidden_state.shape[1:]
     nvar = head_weight.shape[1]
+    mesh_rows = mesh_node_keys.shape[1]
     vpad = -(-nvar // 16) * 16
     cap = send_rows.shape[2]
     slots = n * cap
@@ -379,17 +410,22 @@
     hcols = features // n
     packed = (n, 4 * cap, features // 2)
     vmem = pl.BlockSpec(memory_space=pltpu.VMEM)
-    return pl.pallas_call(
+    hbm = pl.BlockSpec(memory_space=pl.ANY)
+    latent, returned, picks, head = pl.pallas_call(
         functools.partial(kernel, n, m),
         out_shape=(
             jax.ShapeDtypeStruct((1, points, features), BF16),
-            jax.ShapeDtypeStruct(mesh_node_keys.shape, BF16),
-            jax.ShapeDtypeStruct(mesh_node_values.shape, BF16),
-            jax.ShapeDtypeStruct((1, hcols, nvar), F32),
+            jax.ShapeDtypeStruct((2 * n * cap, features), BF16),
+            jax.ShapeDtypeStruct((4 * n * cap, mesh_rows), BF16),
+            jax.ShapeDtypeStruct((nvar, 1, hcols), F32),
         ),
-        in_specs=[vmem] * 12,
-        out_specs=(vmem,) * 4,
+        in_specs=[hbm, vmem, vmem, hbm] + [vmem] * 8,
+        out_specs=(hbm, vmem, vmem, vmem),
         scratch_shapes=[
+            pltpu.VMEM((1, points, features), BF16),
+            pltpu.VMEM(query_weight.shape, BF16),
+            pltpu.VMEM((1, points, features), BF16),
+            pltpu.SemaphoreType.DMA((3,)),
             pltpu.VMEM(packed, BF16),
             pltpu.VMEM(packed, BF16),
             pltpu.VMEM(packed, BF16),
@@ -429,15 +465,29 @@
         mesh_node_keys,
         mesh_node_values,
         query_weight,
-        head_weight,
+        head_weight.T,
         rms_norm_gain.reshape(1, features),
         edge_bias,
         send_rows,
         edge_src,
         targets,
-        point_area_weight.reshape(1, points),
+        point_area_weight,
         variable_loss_weight.reshape(1, nvar),
     )
+    latent, key_grad, value_grad, head = pl.pallas_call(
+        finish,
+        out_shape=(
+            jax.ShapeDtypeStruct((1, points, features), BF16),
+            jax.ShapeDtypeStruct(mesh_node_keys.shape, BF16),
+            jax.ShapeDtypeStruct(mesh_node_values.shape, BF16),
+            jax.ShapeDtypeStruct((nvar, 1, hcols), F32),
+        ),
+        in_specs=[hbm, vmem, vmem, hbm],
+        out_specs=(vmem,) * 4,
+        scratch_shapes=[pltpu.SemaphoreType.DMA((2,))],
+        compiler_params=pltpu.CompilerParams(vmem_limit_bytes=56 * 1024 * 1024),
+    )(latent, returned, picks, head)
+    return latent, key_grad, value_grad, jnp.transpose(head, (1, 2, 0))
 
 
 def solution(mesh):

time: 39 us -> 30.9 us (0.79)
  local copies, waits for them, and re-layouts: 9.16 us -> 0 us
  Pallas kernels: 28.9 us -> 30 us
    unnamed x6 -> x0, local copies, waits for them, and re-layouts: 6.23 us -> none
    pallas_call x0 -> x1, Pallas kernels: none -> 3.07 us  [shards(): pl.pallas_call(finish, out_shape=(jax.ShapeDtypeStruct((1, points, featur...]
    pallas_call x1, Pallas kernels: 28.9 us -> 27 us  [shards(): pl.pallas_call(functools.partial(kernel, n, m), out_shape=(jax.ShapeDtype...]
    pallas_call x1 -> x0, local copies, waits for them, and re-layouts: 1.69 us -> none  [shards(): pl.pallas_call(functools.partial(kernel, n, m), out_shape=(jax.ShapeDtype...]
    reshape x1 -> x0, local copies, waits for them, and re-layouts: 1.25 us -> none  [shards(): point_area_weight.reshape(1, points)]
where the time goes in v2:
time: 30.9 us; the launch traced here: 30.7 us
  Pallas kernels  30 us (97%)
  between operations  0.64 us (2%)
    pallas_call x1, Pallas kernels, shards(): pl.pallas_call(functools.partial(kernel, n, m), out_shape=(jax.ShapeDtype...  27 us
    pallas_call x1, Pallas kernels, shards(): pl.pallas_call(finish, out_shape=(jax.ShapeDtypeStruct((1, points, featur...  3.07 us

profile of v2, /device:TPU:0, one launch (start us, length us, event | category | flops | bytes accessed | tf_op | source)
XLA Modules:
  0.0 30.7 jit_solution(2671846598150936217)
XLA Ops:
  0.6 27.0 %shard_map.147 = (bf16[1,384,1024]{2,1,0:T(8,128)(2,1)}, bf16[32,1024]{1,0:T(8,128)(2,1)}, bf16[64,128]{1,0:T(8,128)(2,1)}, f32[100,1,256]{2,1,0:T(1,128)}) custom-call(bf16[1,384,1024]{2,1,0:T(8,128)(2,1)} %hidden_in.1, bf16[1,128,1024]{2,1,0:T(8,128)(2,1)} %keys.1, bf16[1,128,1024]{2,1,0:T(8,128)(2,1)} %values.1, bf16[1024,1024]{1,0:T(8,128)(2,1)} %wq_in.1, ...), custom_call_target="tpu_custom_call" | custom-call | tf_op jit(solution)/shard_map/pallas_call | solution.py:414
  27.6 3.1 %shard_map.148 = (bf16[1,384,1024]{2,1,0:T(8,128)(2,1)}, bf16[1,128,1024]{2,1,0:T(8,128)(2,1)}, bf16[1,128,1024]{2,1,0:T(8,128)(2,1)}, f32[100,1,256]{2,1,0:T(1,128)}) custom-call(bf16[1,384,1024]{2,1,0:T(8,128)(2,1)} %get-tuple-element.12.latent, bf16[32,1024]{1,0:T(8,128)(2,1)} %get-tuple-element.13.returned, bf16[64,128]{1,0:T(8,128)(2,1)} %get-tuple-element.14.picks, ...), custom_call_target="tpu_custom_call" | custom-call | tf_op jit(solution)/shard_map/pallas_call | solution.py:477

commit v3 on v2

--- a/solution.py
+++ b/solution.py
@@ -51,9 +51,25 @@
     n,
     m,
     hidden_in,
+    keys_in,
+    values_in,
+    wq_in,
+    hw_in,
+    gain_in,
+    bias_in,
+    send_in,
+    edge_in,
+    targets_in,
+    area_in,
+    var_in,
+    out_latent,
+    out_returned,
+    out_picks,
+    out_head,
+    hidden,
     keys,
     values,
-    wq_in,
+    wq,
     hw,
     gain_ref,
     bias,
@@ -62,12 +78,6 @@
     targets,
     area,
     var_weight,
-    out_latent,
-    out_returned,
-    out_picks,
-    out_head,
-    hidden,
-    wq,
     latent,
     local_sems,
     kv_send,
@@ -126,10 +136,27 @@
         pl.semaphore_signal(
             barrier, inc=1, device_id={"mem": lax.rem(member + step, m)}, device_id_type=MESH
         )
-    load_hidden = pltpu.make_async_copy(hidden_in, hidden, local_sems.at[0])
-    load_wq = pltpu.make_async_copy(wq_in, wq, local_sems.at[1])
-    load_hidden.start()
-    load_wq.start()
+    arrays = [
+        (send_in, send_rows),
+        (keys_in, keys),
+        (values_in, values),
+        (hidden_in, hidden),
+        (wq_in, wq),
+        (hw_in, hw),
+        (gain_in, gain_ref),
+        (edge_in, edge_src),
+        (bias_in, bias),
+        (targets_in, targets),
+        (area_in, area),
+        (var_in, var_weight),
+    ]
+    loads = [
+        pltpu.make_async_copy(src, dst, local_sems.at[1 + i]) for i, (src, dst) in enumerate(arrays)
+    ]
+    for load in loads:
+        load.start()
+    for load in loads[:3]:
+        load.wait()
 
     table = send_rows[0].astype(F32).astype(BF16)
     spread_rows = jnp.where(iota((rows, n), 0) // pair == iota((rows, n), 1), 1.0, 0.0).astype(BF16)
@@ -163,6 +190,8 @@
         copy.start()
     kv_recv[me] = kv_send[me]
 
+    for load in loads[3:]:
+        load.wait()
     hwt[...] = jnp.zeros_like(hwt)
     hwt[:nvar, :] = hw[...]
     kb[...] = jnp.zeros_like(kb)
@@ -176,8 +205,6 @@
         keepdims=True,
     )
 
-    load_hidden.wait()
-    load_wq.wait()
     q_ref[...] = mm(hidden[0], wq[...]).astype(BF16)
 
     for copy in kv_copies:
@@ -346,7 +373,7 @@
         at = slice(c * LANES, (c + 1) * LANES)
         latent[0, at, :] = (gc_ref[at, :] + mm(gs_ref[:, at], kbw[...], 0, 0)).astype(BF16)
 
-    store_latent = pltpu.make_async_copy(latent, out_latent, local_sems.at[2])
+    store_latent = pltpu.make_async_copy(latent, out_latent, local_sems.at[0])
     store_latent.start()
 
     for copy in hw_copies:
@@ -370,18 +397,27 @@
             copy.wait_send()
 
 
-def finish(latent, returned, picks, head, out_latent, out_keys, out_values, out_head, sems):
-    copies = [
-        pltpu.make_async_copy(latent, out_latent, sems.at[0]),
-        pltpu.make_async_copy(head, out_head, sems.at[1]),
-    ]
-    for copy in copies:
-        copy.start()
+def finish(
+    latent, returned, picks, head, out_latent, out_keys, out_values, out_head, held, sems
+):
+    parts = held.shape[0]
+    height = held.shape[1]
+    loads, stores = [], []
+    for i in range(parts):
+        at = pl.ds(i * height, height)
+        loads.append(pltpu.make_async_copy(latent.at[0, at], held.at[i], sems.at[0, i]))
+        stores.append(pltpu.make_async_copy(held.at[i], out_latent.at[0, at], sems.at[1, i]))
+    for load in loads:
+        load.start()
     rows = returned.shape[0]
     out_keys[0] = mm(picks[:rows], returned[...], 0, 0).astype(BF16)
     out_values[0] = mm(picks[rows:], returned[...], 0, 0).astype(BF16)
-    for copy in copies:
-        copy.wait()
+    out_head[...] = head[...]
+    for load, store in zip(loads, stores):
+        load.wait()
+        store.start()
+    for store in stores:
+        store.wait()
 
 
 def shards(
@@ -411,6 +447,20 @@
     packed = (n, 4 * cap, features // 2)
     vmem = pl.BlockSpec(memory_space=pltpu.VMEM)
     hbm = pl.BlockSpec(memory_space=pl.ANY)
+    operands = (
+        grid_hidden_state,
+        mesh_node_keys,
+        mesh_node_values,
+        query_weight,
+        head_weight.T,
+        rms_norm_gain.reshape(1, features),
+        edge_bias,
+        send_rows,
+        edge_src,
+        targets,
+        point_area_weight,
+        variable_loss_weight.reshape(1, nvar),
+    )
     latent, returned, picks, head = pl.pallas_call(
         functools.partial(kernel, n, m),
         out_shape=(
@@ -419,13 +469,12 @@
             jax.ShapeDtypeStruct((4 * n * cap, mesh_rows), BF16),
             jax.ShapeDtypeStruct((nvar, 1, hcols), F32),
         ),
-        in_specs=[hbm, vmem, vmem, hbm] + [vmem] * 8,
+        in_specs=[hbm] * 12,
         out_specs=(hbm, vmem, vmem, vmem),
         scratch_shapes=[
+            *[pltpu.VMEM(a.shape, a.dtype) for a in operands],
             pltpu.VMEM((1, points, features), BF16),
-            pltpu.VMEM(query_weight.shape, BF16),
-            pltpu.VMEM((1, points, features), BF16),
-            pltpu.SemaphoreType.DMA((3,)),
+            pltpu.SemaphoreType.DMA((1 + len(operands),)),
             pltpu.VMEM(packed, BF16),
             pltpu.VMEM(packed, BF16),
             pltpu.VMEM(packed, BF16),
@@ -460,20 +509,7 @@
         compiler_params=pltpu.CompilerParams(
             collective_id=0, has_side_effects=True, vmem_limit_bytes=56 * 1024 * 1024
         ),
-    )(
-        grid_hidden_state,
-        mesh_node_keys,
-        mesh_node_values,
-        query_weight,
-        head_weight.T,
-        rms_norm_gain.reshape(1, features),
-        edge_bias,
-        send_rows,
-        edge_src,
-        targets,
-        point_area_weight,
-        variable_loss_weight.reshape(1, nvar),
-    )
+    )(*operands)
     latent, key_grad, value_grad, head = pl.pallas_call(
         finish,
         out_shape=(
@@ -482,9 +518,12 @@
             jax.ShapeDtypeStruct(mesh_node_values.shape, BF16),
             jax.ShapeDtypeStruct((nvar, 1, hcols), F32),
         ),
-        in_specs=[hbm, vmem, vmem, hbm],
-        out_specs=(vmem,) * 4,
-        scratch_shapes=[pltpu.SemaphoreType.DMA((2,))],
+        in_specs=[hbm, vmem, vmem, vmem],
+        out_specs=(hbm, vmem, vmem, vmem),
+        scratch_shapes=[
+            pltpu.VMEM((chunks, LANES, features), BF16),
+            pltpu.SemaphoreType.DMA((2, chunks)),
+        ],
         compiler_params=pltpu.CompilerParams(vmem_limit_bytes=56 * 1024 * 1024),
     )(latent, returned, picks, head)
     return latent, key_grad, value_grad, jnp.transpose(head, (1, 2, 0))

time: 30.9 us -> 30.3 us (0.981)
  Pallas kernels: 30 us -> 29.5 us
    pallas_call x1, Pallas kernels: 27 us -> 25.8 us  [shards(): pl.pallas_call(functools.partial(kernel, n, m), out_shape=(jax.ShapeDtype...]
    pallas_call x1, Pallas kernels: 3.07 us -> 3.68 us  [shards(): pl.pallas_call(finish, out_shape=(jax.ShapeDtypeStruct((1, points, featur...]
where the time goes in v3:
time: 30.3 us; the launch traced here: 30.2 us
  Pallas kernels  29.5 us (97%)
  between operations  0.64 us (2%)
    pallas_call x1, Pallas kernels, shards(): pl.pallas_call(functools.partial(kernel, n, m), out_shape=(jax.ShapeDtype...  25.8 us
    pallas_call x1, Pallas kernels, shards(): pl.pallas_call(finish, out_shape=(jax.ShapeDtypeStruct((1, points, featur...  3.68 us

profile of v3, /device:TPU:0, one launch (start us, length us, event | category | flops | bytes accessed | tf_op | source)
XLA Modules:
  0.0 30.2 jit_solution(8959443942767491949)
XLA Ops:
  0.6 25.8 %shard_map.147 = (bf16[1,384,1024]{2,1,0:T(8,128)(2,1)}, bf16[32,1024]{1,0:T(8,128)(2,1)}, bf16[64,128]{1,0:T(8,128)(2,1)}, f32[100,1,256]{2,1,0:T(1,128)}) custom-call(bf16[1,384,1024]{2,1,0:T(8,128)(2,1)} %hidden_in.1, bf16[1,128,1024]{2,1,0:T(8,128)(2,1)} %keys_in.1, bf16[1,128,1024]{2,1,0:T(8,128)(2,1)} %values_in.1, bf16[1024,1024]{1,0:T(8,128)(2,1)} %wq_in.1, ...), custom_call_target="tpu_custom_call" | custom-call | tf_op jit(solution)/shard_map/pallas_call | solution.py:464
  26.5 3.7 %shard_map.148 = (bf16[1,384,1024]{2,1,0:T(8,128)(2,1)}, bf16[1,128,1024]{2,1,0:T(8,128)(2,1)}, bf16[1,128,1024]{2,1,0:T(8,128)(2,1)}, f32[100,1,256]{2,1,0:T(1,128)}) custom-call(bf16[1,384,1024]{2,1,0:T(8,128)(2,1)} %get-tuple-element.12.latent, bf16[32,1024]{1,0:T(8,128)(2,1)} %get-tuple-element.13.returned, bf16[64,128]{1,0:T(8,128)(2,1)} %get-tuple-element.14.picks, ...), custom_call_target="tpu_custom_call" | custom-call | tf_op jit(solution)/shard_map/pallas_call | solution.py:513
